TPU v7x, 32 devices: a whole 2x2x4 slice. The times are simulated.
32 devices in a mesh: member: 2 (over y), wave: 4 (over z), level: 2 (over x), fld: 2 (over core).
Axes of the slice: x: 2, y: 2, z: 4, core: 2. Of those that a mesh axis runs over, the one named last changes fastest.
Arguments:
- grid_state: bfloat16 [256, 2, 256, 1536], P(('member', 'level'), 'fld', 'wave'), parts along dimension 0, may hold values from -6 to 6
- legendre: bfloat16 [512, 2, 256, 256], P(('wave', 'level'), 'fld'), may hold values from -0.375 to 0.375
- wave_order: int32 [512], replicated, may hold values from 0 to 511, each once
- lat_order: int32 [256], replicated, may hold values from 0 to 255, each once
- eig_rates: float32 [128], replicated, may hold values from 0.1 to 4
- modes_in: bfloat16 [128, 128], replicated, may hold values from -0.5 to 0.5
- modes_out: bfloat16 [128, 128], replicated, may hold values from -0.5 to 0.5
Outputs:
- new_state: bfloat16 [256, 2, 256, 1536], P(('member', 'level'), 'fld', 'wave'), parts along dimension 0
There are 2 independent parts, one for each index of `member`. A program takes and returns all parts, laid end to end along the dimension named above; an argument that names none is the same for every part. Nothing has to cross between parts.
Inputs may be any that keep to these rules, and one draw needn't show every extreme that they name: Slot s holds zonal wavenumber wave_order[s]; every wavenumber 0 to 511 is held by exactly one slot. Latitude row r lies at Gaussian latitude index lat_order[r] counted from the equator, the same in both hemispheres; every index appears once.
All inputs are finite; a program needn't handle non-finite values.
Results may differ from a plain program's by a relative error of at most 0.0098.
Values may be sent and summed in bfloat16 or wider, within the bound.
A program may use at most 128 MiB of HBM per device.

v0:
```python
import math

import jax
import jax.numpy as jnp
from jax import lax
from jax.sharding import PartitionSpec as P

tau_scale = 2.0


def partner(value, axis, stride):
    mask = 2**stride
    pairs = [(source, source ^ mask) for source in range(lax.axis_size(axis))]
    return lax.ppermute(value, axis, pairs)


def fourier_table(wave_order, lon_count):
    longitude = jnp.arange(lon_count, dtype=jnp.int32)
    phase_index = longitude[:, None] * wave_order[None, :] % lon_count
    angles = phase_index.astype(jnp.float32) * (2.0 * math.pi / lon_count)
    weight_scale = math.sqrt(2.0 / lon_count)
    return jnp.concatenate(
        [jnp.cos(angles) * weight_scale, -jnp.sin(angles) * weight_scale], axis=1
    ).astype(jnp.bfloat16)


def degrees(wave_ids, parity, half_count):
    return wave_ids[:, None] + 2 * jnp.arange(half_count, dtype=jnp.int32)[None, :] + parity


def triangle_mask(wave_ids, parity, half_count, wave_count):
    return (degrees(wave_ids, parity, half_count) <= wave_count - 1).astype(jnp.float32)


def damping(wave_ids, parity, half_count, wave_count, eig_rates):
    degree_f = degrees(wave_ids, parity, half_count).astype(jnp.float32)
    damp_ratio = tau_scale * degree_f * (degree_f + 1.0) / float(wave_count * (wave_count - 1))
    return 1.0 / (1.0 + damp_ratio[:, :, None] * eig_rates[None, None, :])


def forward_legendre(mirrored, table_part, in_triangle):
    spectral = jnp.einsum(
        "lhrcs,shrj->sjcl", mirrored, table_part, preferred_element_type=jnp.float32
    )
    return (spectral * in_triangle[:, :, None, None]).astype(jnp.bfloat16)


def inverse_legendre(solved, table_part):
    return jnp.einsum(
        "sjcl,shrj->lhrcs", solved, table_part, preferred_element_type=jnp.float32
    ).astype(jnp.bfloat16)


def implicit_solve(columns, factor, modes_in, modes_out):
    modal = jnp.einsum("sjcl,kl->sjck", columns, modes_in, preferred_element_type=jnp.float32)
    modal = (modal * factor[:, :, None, :]).astype(jnp.bfloat16)
    return jnp.einsum("sjck,lk->sjcl", modal, modes_out, preferred_element_type=jnp.float32).astype(
        jnp.bfloat16
    )


def shards(grid_state, legendre, wave_order, lat_order, eig_rates, modes_in, modes_out):
    lon_count = grid_state.shape[3]
    rows_here = grid_state.shape[2]
    wave_count = wave_order.shape[0]
    half_rows = lat_order.shape[0]
    half_count = legendre.shape[3]
    wave_size = lax.axis_size("wave")
    level_size = lax.axis_size("level")
    parity = lax.axis_index("fld")
    wave_place = lax.axis_index("wave")
    level_place = lax.axis_index("level")
    wave_table = fourier_table(wave_order, lon_count)
    lat_rows = lax.dynamic_slice_in_dim(lat_order, wave_place * rows_here, rows_here)
    sine = jnp.sin((lat_rows.astype(jnp.float32) + 0.5) * (math.pi / (2.0 * half_rows)))
    hemi_sign = 1.0 - 2.0 * parity.astype(jnp.float32)
    coupling = (0.5 * hemi_sign * sine)[None, None, :, None]
    wide_count = wave_count // wave_size
    narrow_count = wide_count // level_size
    wide_start = wave_place * wide_count
    narrow_start = wide_start + level_place * narrow_count
    wide_waves = lax.dynamic_slice_in_dim(wave_order, wide_start, wide_count)
    narrow_waves = lax.dynamic_slice_in_dim(wave_order, narrow_start, narrow_count)
    factor = damping(narrow_waves, parity, half_count, wave_count, eig_rates)
    wide_table = lax.all_gather(legendre, "level", axis=0, tiled=True)
    wide_mask = triangle_mask(wide_waves, parity, half_count, wave_count)
    initial = grid_state.astype(jnp.float32)
    current = grid_state
    forcing = (initial + coupling * jnp.tanh(current.astype(jnp.float32))).astype(jnp.bfloat16)
    fourier_rows = jnp.einsum(
        "lhrg,gk->lhrk", forcing, wave_table, preferred_element_type=jnp.float32
    )
    fourier_rows = fourier_rows.astype(jnp.bfloat16).reshape(
        fourier_rows.shape[:3] + (2, wave_count)
    )
    mirror_part = partner(fourier_rows, "fld", 0)
    mirrored = (
        mirror_part.astype(jnp.float32) + hemi_sign * fourier_rows.astype(jnp.float32)
    ).astype(jnp.bfloat16)
    gathered = lax.all_to_all(mirrored, "wave", split_axis=4, concat_axis=2, tiled=True)
    spectral = forward_legendre(gathered, wide_table, wide_mask)
    columns = lax.all_to_all(spectral, "level", split_axis=0, concat_axis=3, tiled=True)
    solved = implicit_solve(columns, factor, modes_in, modes_out)
    level_rows = lax.all_to_all(solved, "level", split_axis=3, concat_axis=0, tiled=True)
    grid_coeffs = inverse_legendre(level_rows, wide_table)
    grid_coeffs = lax.all_to_all(grid_coeffs, "wave", split_axis=2, concat_axis=4, tiled=True)
    mirror_back = partner(grid_coeffs, "fld", 0)
    hemi_grid = (
        0.5 * (mirror_back.astype(jnp.float32) + hemi_sign * grid_coeffs.astype(jnp.float32))
    ).astype(jnp.bfloat16)
    flat_coeffs = hemi_grid.reshape(hemi_grid.shape[:3] + (2 * wave_count,))
    current = jnp.einsum(
        "lhrk,gk->lhrg", flat_coeffs, wave_table, preferred_element_type=jnp.float32
    ).astype(jnp.bfloat16)
    return current


def solution(mesh):
    placed = (
        P(("member", "level"), "fld", "wave", None),
        P(("wave", "level"), "fld", None, None),
        P(),
        P(),
        P(),
        P(),
        P(),
    )
    return jax.shard_map(
        shards,
        mesh=mesh,
        in_specs=placed,
        out_specs=P(("member", "level"), "fld", "wave", None),
        check_vma=False,
    )
```

profile of v0, /device:TPU:0, one launch (start us, length us, event | category | flops | bytes accessed | tf_op | source)
XLA Modules:
  0.0 995.6 jit_solution(6568454296517900749)
XLA Ops:
  6.5 0.0 copy-start
  6.5 0.0 all-gather.2.cloned.1.call-start
  6.5 14.1 %multiply_convert_fusion.4 = (bf16[1536,512]{1,0:T(8,128)(2,1)S(1)}, bf16[1536,512]{1,0:T(8,128)(2,1)S(1)}) fusion(s32[512]{0:T(512)} %param.9), kind=kLoop, calls=%fused_computation.28 | loop fusion | flops 11010048 | bytes 3147776 | tf_op jit(solution)/shard_map/convert
  20.6 0.0 copy-start.2
  20.7 0.0 copy-start.4
  20.7 0.8 sine_multiply_fusion
  21.5 18.9 %fusion.13 = bf16[64,64,1024]{2,1,0:T(8,128)(2,1)} fusion(bf16[64,1,64,1536]{3,2,1,0:T(8,128)(2,1)} %param.7, f32[64]{0:T(128)S(1)} %sine_multiply_fusion, bf16[1536,512]{1,0:T(8,128)(2,1)S(1)} %get-tuple-element.6, bf16[1536,512]{1,0:T(8,128)(2,1)S(1)} %get-tuple-element.5), kind=kOutput, calls=%fused_computation.21 | convolution fusion | flops 12920553472 | bytes 24117504 | tf_op jit(solution)/shard_map/lhrg,gk->lhrk/dot_general | solution.py:90
  40.4 0.0 copy-done.2
  40.4 0.0 copy-done.4
  40.4 14.5 %reshape.138 = bf16[64,1,64,2,512]{4,3,2,0,1:T(2,128)(2,1)} reshape(bf16[64,64,1024]{2,1,0:T(8,128)(2,1)} %fusion.13) | data formatting | bytes 16777216 | tf_op jit(solution)/shard_map/reshape | solution.py:93
  54.9 9.0 copy.61
  64.0 0.5 collective-permute-start
  64.4 0.0 all-gather.2.cloned.1.call-update
  64.4 13.1 %collective-permute-done = bf16[64,1,64,2,512]{4,2,3,0,1:T(8,128)(2,1)} collective-permute-done((bf16[64,1,64,2,512]{4,2,3,0,1:T(8,128)(2,1)}, bf16[64,1,64,2,512]{4,2,3,0,1:T(8,128)(2,1)}, u32[]{:S(2)}, u32[]{:S(2)}) %collective-permute-start) | collective-permute-done | bytes 8388640 | tf_op jit(solution)/shard_map/ppermute | solution.py:14
  77.5 12.1 %add_convert_fusion = bf16[64,1,64,2,512]{4,2,3,0,1:T(8,128)(2,1)} fusion(bf16[64,1,64,2,512]{4,2,3,0,1:T(8,128)(2,1)} %collective-permute-done, f32[]{:T(128)S(6)} %sub.3, bf16[64,1,64,2,512]{4,3,2,0,1:T(2,128)(2,1)} %reshape.138), kind=kLoop, calls=%fused_computation.11 | loop fusion | flops 20971520 | bytes 25165828 | tf_op jit(solution)/shard_map/convert_element_type | solution.py:99
  89.7 34.4 %copy.63 = bf16[64,1,64,2,512]{2,3,0,1,4:T(2,128)(2,1)} copy(bf16[64,1,64,2,512]{4,2,3,0,1:T(8,128)(2,1)} %add_convert_fusion) | data formatting | bytes 16777216 | tf_op jit(solution)/shard_map/convert_element_type | solution.py:99
  124.1 16.8 %reshape.146 = bf16[4,2,524288]{2,1,0:T(2,128)(2,1)} reshape(bf16[512,1,64,2,64]{4,3,2,1,0:T(2,128)(2,1)} %bitcast.76) | data formatting | bytes 16777216
  140.9 0.0 copy-start.7
  140.9 6.2 all-to-all-start
  147.1 0.0 copy-done.7
  147.1 0.1 dynamic_slice.10
  147.2 0.1 fusion.26
  147.3 184.2 %all-to-all-done = bf16[4,2,524288]{2,1,0:T(2,128)(2,1)} async-done(((bf16[4,2,524288]{2,1,0:T(2,128)(2,1)}), bf16[4,2,524288]{2,1,0:T(2,128)(2,1)}, u32[]{:S(2)}, u32[]{:S(2)}) %all-to-all-start) | async-done | bytes 8388640 | tf_op jit(solution)/shard_map/all_to_all | solution.py:100
  331.5 16.0 %reshape.147 = bf16[512,1,64,2,64]{4,3,2,1,0:T(2,128)(2,1)} reshape(bf16[4,2,524288]{2,1,0:T(2,128)(2,1)} %all-to-all-done) | data formatting | bytes 16777216
  347.5 41.2 %copy.81 = bf16[64,1,64,2,4,128]{5,4,2,3,0,1:T(4,128)(2,1)} copy(bf16[64,1,64,2,4,128]{2,3,0,5,4,1:T(2,128)(2,1)} %bitcast.77) | data formatting | bytes 16777216 | tf_op jit(solution)/shard_map/all_to_all | solution.py:100
  388.6 9.3 copy.65
  398.0 12.1 %copy.66 = bf16[64,256,2,128]{1,0,2,3:T(8,128)(2,1)} copy(bf16[64,256,2,128]{3,1,2,0:T(8,128)(2,1)} %bitcast.81) | data formatting | bytes 16777216 | tf_op jit(solution)/shard_map/reshape.6
  410.1 0.0 all-gather.2.cloned.1.call-done
  410.1 15.1 %fusion.18 = bf16[128,256,2,64]{1,3,2,0:T(8,128)(2,1)} fusion(f32[128,256]{1,0:T(8,128)S(1)} %fusion.26, bf16[64,256,2,128]{1,0,2,3:T(8,128)(2,1)} %copy.66, bf16[128,1,256,256]{3,2,1,0:T(8,128)(2,1)} %all-gather.2.cloned.1.call-done), kind=kOutput, calls=%fused_computation.22 | convolution fusion | flops 2155872256 | bytes 33685504 | tf_op jit(solution)/shard_map/lhrcs,shrj->sjcl/dot_general | solution.py:42
  425.2 0.0 copy-start.8
  425.2 7.1 all-to-all-start.1
  432.3 0.1 dynamic_slice.11
  432.4 0.1 multiply_multiply_fusion
  432.5 0.0 copy-done.8
  432.5 15.2 %add_divide_fusion = f32[64,256,128]{2,1,0:T(8,128)} fusion(f32[128]{0:T(128)S(1)} %copy-done.8, f32[64,256]{1,0:T(8,128)S(1)} %multiply_multiply_fusion), kind=kLoop, calls=%fused_computation.19 | loop fusion | flops 6291456 | bytes 8454656 | tf_op jit(solution)/shard_map/div | solution.py:38
  447.7 77.0 %all-to-all-done.1 = bf16[128,256,2,64]{1,3,2,0:T(8,128)(2,1)} async-done(((bf16[128,256,2,64]{1,3,2,0:T(8,128)(2,1)}), bf16[128,256,2,64]{1,3,2,0:T(8,128)(2,1)}, u32[]{:S(2)}, u32[]{:S(2)}) %all-to-all-start.1) | async-done | bytes 8388640 | tf_op jit(solution)/shard_map/all_to_all | solution.py:102
  524.7 0.0 copy-start.6
  524.7 8.4 copy.67
  533.1 0.0 copy-done
  533.1 0.0 copy-done.6
  533.2 10.6 %convolution_convert_fusion.1 = bf16[64,256,2,128]{3,1,2,0:T(8,128)(2,1)} fusion(bf16[64,256,2,128]{1,3,2,0:T(8,128)(2,1)} %bitcast.79, f32[64,256,128]{2,1,0:T(8,128)} %add_divide_fusion, bf16[128,128]{1,0:T(8,128)(2,1)S(1)} %copy-done, bf16[128,128]{1,0:T(8,128)(2,1)S(1)} %copy-done.6), kind=kOutput, calls=%fused_computation.20 | convolution fusion | flops 2160066560 | bytes 25231360 | tf_op jit(solution)/shard_map/sjck,lk->sjcl/dot_general | solution.py:57
  543.7 21.1 %copy.69 = bf16[64,256,2,128]{1,2,0,3:T(2,128)(2,1)} copy(bf16[64,256,2,128]{3,1,2,0:T(8,128)(2,1)} %convolution_convert_fusion.1) | data formatting | bytes 16777216 | tf_op jit(solution)/shard_map/convert_element_type | solution.py:57
  564.8 102.5 %all_to_all.69 = bf16[64,256,2,128]{1,2,0,3:T(2,128)(2,1)} all-to-all(bf16[64,256,2,128]{1,2,0,3:T(2,128)(2,1)} %copy.69), channel_id=1, replica_groups=mesh['member'=2,'wave'=4,'level'=2,'fld'=2] {'level'}, dimensions={3} | all-to-all | bytes 16777216 | tf_op jit(solution)/shard_map/all_to_all | solution.py:104
  667.3 15.9 %copy.70 = bf16[64,256,2,128]{1,3,2,0:T(8,128)(2,1)} copy(bf16[64,256,2,128]{1,2,0,3:T(2,128)(2,1)} %all_to_all.69) | data formatting | bytes 16777216 | tf_op jit(solution)/shard_map/all_to_all | solution.py:104
  683.2 8.3 copy.71
  691.5 13.3 %convert_bitcast_fusion = bf16[64,1,256,2,128]{2,0,3,4,1:T(8,128)(2,1)} fusion(bf16[128,256,2,64]{1,3,2,0:T(8,128)(2,1)} %bitcast.78, bf16[128,1,256,256]{3,2,1,0:T(8,128)(2,1)} %all-gather.2.cloned.1.call-done), kind=kOutput, calls=%fused_computation.18 | convolution fusion | flops 2151677952 | bytes 33554432 | tf_op jit(solution)/shard_map/sjcl,shrj->lhrcs/dot_general | solution.py:49
  704.8 13.5 %copy.72 = bf16[64,1,256,2,128]{4,0,3,1,2:T(8,128)(2,1)} copy(bf16[64,1,256,2,128]{2,0,3,4,1:T(8,128)(2,1)} %convert_bitcast_fusion) | data formatting | bytes 16777216 | tf_op jit(solution)/shard_map/convert_element_type | solution.py:51
  718.3 188.7 %all_to_all.70 = bf16[64,1,256,2,128]{4,0,3,1,2:T(8,128)(2,1)} all-to-all(bf16[64,1,256,2,128]{4,0,3,1,2:T(8,128)(2,1)} %copy.72), channel_id=1, replica_groups=mesh['member'=2,'wave'=4,'level'=2,'fld'=2] {'wave'}, dimensions={2} | all-to-all | bytes 16777216 | tf_op jit(solution)/shard_map/all_to_all | solution.py:106
  907.0 12.2 %copy.73 = bf16[64,1,256,2,128]{4,2,3,0,1:T(8,128)(2,1)} copy(bf16[64,1,256,2,128]{4,0,3,1,2:T(8,128)(2,1)} %all_to_all.70) | data formatting | bytes 16777216 | tf_op jit(solution)/shard_map/all_to_all | solution.py:106
  919.2 8.4 copy.87
  927.6 0.0 collective-permute-start.1
  927.6 13.4 %collective-permute-done.1 = bf16[64,1,64,2,512]{4,2,3,0,1:T(8,128)(2,1)S(1)} collective-permute-done((bf16[64,1,64,2,512]{4,2,3,0,1:T(8,128)(2,1)}, bf16[64,1,64,2,512]{4,2,3,0,1:T(8,128)(2,1)S(1)}, u32[]{:S(2)}, u32[]{:S(2)}) %collective-permute-start.1) | collective-permute-done | bytes 8388640 | tf_op jit(solution)/shard_map/ppermute | solution.py:14
  941.0 5.7 multiply_convert_fusion
  946.7 7.7 copy.75
  954.5 0.0 copy-start.3
  954.5 0.0 copy-start.5
  954.5 14.5 %reshape.141 = bf16[64,64,1024]{2,1,0:T(8,128)(2,1)} reshape(bf16[64,1,64,2,512]{4,3,2,0,1:T(2,128)(2,1)} %copy.75) | data formatting | bytes 16777216 | tf_op jit(solution)/shard_map/reshape.9
  968.9 0.0 copy-done.3
  968.9 0.0 copy-done.5
  968.9 0.0 copy-start.1
  968.9 19.4 %fusion.10 = bf16[64,1,64,1536]{3,2,1,0:T(8,128)(2,1)} fusion(bf16[64,64,1024]{2,1,0:T(8,128)(2,1)} %reshape.141, bf16[1536,512]{1,0:T(8,128)(2,1)S(1)} %copy-done.5, bf16[1536,512]{1,0:T(8,128)(2,1)S(1)} %copy-done.3), kind=kOutput, calls=%fused_computation.16 | convolution fusion | flops 12897484800 | bytes 24117248 | tf_op jit(solution)/shard_map/lhrk,gk->lhrg/dot_general | solution.py:112
  988.3 0.0 copy-done.1
  (1 shorter events, 0.0 us)
Async XLA Ops:
  6.5 526.6 %copy-start = (bf16[128,128]{1,0:T(8,128)(2,1)S(1)}, bf16[128,128]{1,0:T(8,128)(2,1)}, u32[]{:S(2)}) copy-start(bf16[128,128]{1,0:T(8,128)(2,1)} %param.13) | copy-start | bytes 98308
  6.5 403.6 %all-gather.2.cloned.1.call-start = ((), (), s32[]{:S(2)}) async-start(), calls=%async_computation.4 | async-start | bytes 25165824 | tf_op jit(solution)/shard_map/all_gather | solution.py:85
  20.6 19.8 %copy-start.2 = (bf16[1536,512]{1,0:T(8,128)(2,1)}, bf16[1536,512]{1,0:T(8,128)(2,1)S(1)}, u32[]{:S(2)}) copy-start(bf16[1536,512]{1,0:T(8,128)(2,1)S(1)} %get-tuple-element.5) | copy-start | bytes 4718596
  20.7 19.8 %copy-start.4 = (bf16[1536,512]{1,0:T(8,128)(2,1)}, bf16[1536,512]{1,0:T(8,128)(2,1)S(1)}, u32[]{:S(2)}) copy-start(bf16[1536,512]{1,0:T(8,128)(2,1)S(1)} %get-tuple-element.6) | copy-start | bytes 4718596
  64.0 13.6 %collective-permute-start = (bf16[64,1,64,2,512]{4,2,3,0,1:T(8,128)(2,1)}, bf16[64,1,64,2,512]{4,2,3,0,1:T(8,128)(2,1)}, u32[]{:S(2)}, u32[]{:S(2)}) collective-permute-start(bf16[64,1,64,2,512]{4,2,3,0,1:T(8,128)(2,1)} %copy.61), channel_id=1, source_target_pairs={{0,1},{1,0},{2,3},{3,2},{4,5},{5,4},{6,7},{7,6},{8,9},{9,8},{10,11... | collective-permute-start | bytes 25165832 | tf_op jit(solution)/shard_map/ppermute | solution.py:14
  140.9 6.2 copy-start.7
  140.9 190.6 %all-to-all-start = ((bf16[4,2,524288]{2,1,0:T(2,128)(2,1)}), bf16[4,2,524288]{2,1,0:T(2,128)(2,1)}, u32[]{:S(2)}, u32[]{:S(2)}) async-start(bf16[4,2,524288]{2,1,0:T(2,128)(2,1)} %reshape.146), calls=%async_computation | async-start | bytes 16777216 | tf_op jit(solution)/shard_map/all_to_all | solution.py:100
  425.2 7.3 copy-start.8
  425.2 99.5 %all-to-all-start.1 = ((bf16[128,256,2,64]{1,3,2,0:T(8,128)(2,1)}), bf16[128,256,2,64]{1,3,2,0:T(8,128)(2,1)}, u32[]{:S(2)}, u32[]{:S(2)}) async-start(bf16[128,256,2,64]{1,3,2,0:T(8,128)(2,1)} %fusion.18), calls=%async_computation.1 | async-start | bytes 16777216 | tf_op jit(solution)/shard_map/all_to_all | solution.py:102
  524.7 8.5 copy-start.6
  927.6 13.4 %collective-permute-start.1 = (bf16[64,1,64,2,512]{4,2,3,0,1:T(8,128)(2,1)}, bf16[64,1,64,2,512]{4,2,3,0,1:T(8,128)(2,1)S(1)}, u32[]{:S(2)}, u32[]{:S(2)}) collective-permute-start(bf16[64,1,64,2,512]{4,2,3,0,1:T(8,128)(2,1)} %bitcast.83), channel_id=1, source_target_pairs={{0,1},{1,0},{2,3},{3,2},{4,5},{5,4},{6,7},{7,6},{8,9},{9,8},{10,11... | collective-permute-start | bytes 25165832 | tf_op jit(solution)/shard_map/ppermute | solution.py:14
  954.5 14.5 %copy-start.3 = (bf16[1536,512]{1,0:T(8,128)(2,1)S(1)}, bf16[1536,512]{1,0:T(8,128)(2,1)}, u32[]{:S(2)}) copy-start(bf16[1536,512]{1,0:T(8,128)(2,1)} %copy-done.2) | copy-start | bytes 4718596
  954.5 14.5 %copy-start.5 = (bf16[1536,512]{1,0:T(8,128)(2,1)S(1)}, bf16[1536,512]{1,0:T(8,128)(2,1)}, u32[]{:S(2)}) copy-start(bf16[1536,512]{1,0:T(8,128)(2,1)} %copy-done.4) | copy-start | bytes 4718596
  968.9 19.4 %copy-start.1 = (bf16[128,128]{1,0:T(8,128)(2,1)S(1)}, bf16[128,128]{1,0:T(8,128)(2,1)}, u32[]{:S(2)}) copy-start(bf16[128,128]{1,0:T(8,128)(2,1)} %param.13) | copy-start | bytes 98308
Sparse Core Ops, SparseCore 0:
  64.6 201.2 all-gather.1
where the time goes:
time: 1010 us; the launch traced here: 996 us
  blocking collectives  291 us (29%)
  waiting for transfers between devices  288 us (29%)
  local copies, waits for them, and re-layouts  264 us (26%)
  matrix products  77.3 us (8%)
  other arithmetic  48.2 us (5%)
  between operations  13.9 us (1%)
  starting transfers between devices  13.8 us (1%)
    all_to_all x1, blocking collectives, shards(): lax.all_to_all(grid_coeffs, 'wave', split_axis=2, concat_axis=4, tiled=True)  189 us
    all_to_all x1, waiting for transfers between devices, shards(): lax.all_to_all(mirrored, 'wave', split_axis=4, concat_axis=2, tiled=True)  184 us
    all_to_all x1, blocking collectives, shards(): lax.all_to_all(solved, 'level', split_axis=3, concat_axis=0, tiled=True)  102 us
    all_to_all x1, waiting for transfers between devices, shards(): lax.all_to_all(spectral, 'level', split_axis=0, concat_axis=3, tiled=True)  77 us
    all_to_all x2, local copies, waits for them, and re-layouts, shards(): lax.all_to_all(mirrored, 'wave', split_axis=4, concat_axis=2, tiled=True)  50.5 us
    convert_element_type x1, local copies, waits for them, and re-layouts, shards(): mirrored = (mirror_part.astype(jnp.float32) + hemi_sign * fourier_rows.as...  34.4 us
    unnamed x20, local copies, waits for them, and re-layouts  32.8 us
    another operation x2, local copies, waits for them, and re-layouts  26.6 us
  transfers between devices with their start and end apart: 5, of which 4 were waited for; matrix products, arithmetic and copies ran while one was open for 16% of the time, Pallas kernels for 0%

commit v1 on v0

--- a/solution.py
+++ b/solution.py
@@ -1,9 +1,19 @@
+import functools
 import math
 
 import jax
 import jax.numpy as jnp
+import numpy as np
 from jax import lax
+from jax.experimental import pallas as pl
+from jax.experimental.pallas import tpu as pltpu
 from jax.sharding import PartitionSpec as P
+
+LANES = 128
+PACK = 16
+SLOT_CHUNKS = 1
+SLOTS_PER_STEP = 4
+VMEM = 60 * 1024 * 1024
 
 tau_scale = 2.0
 
@@ -59,7 +69,7 @@
     )
 
 
-def shards(grid_state, legendre, wave_order, lat_order, eig_rates, modes_in, modes_out):
+def general_shards(grid_state, legendre, wave_order, lat_order, eig_rates, modes_in, modes_out):
     lon_count = grid_state.shape[3]
     rows_here = grid_state.shape[2]
     wave_count = wave_order.shape[0]
@@ -115,6 +125,295 @@
     return current
 
 
+def selected_table(wave_order, lon_count):
+    wave_count = wave_order.shape[0]
+    phase = np.arange(wave_count)[:, None] * np.arange(lon_count)[None, :] % lon_count
+    angles = phase * (2.0 * math.pi / lon_count)
+    rows = np.stack([np.cos(angles), -np.sin(angles)], axis=1) * math.sqrt(2.0 / lon_count)
+    rows = jnp.asarray(rows.reshape(2 * wave_count, lon_count).astype(np.float32), jnp.bfloat16)
+    wanted = 2 * wave_order[:, None] + jnp.arange(2, dtype=jnp.int32)[None, :]
+    held = jnp.arange(2 * wave_count, dtype=jnp.int32)
+    pick = (wanted.reshape(-1, 1) == held[None, :]).astype(jnp.bfloat16)
+    return jnp.dot(pick, rows, preferred_element_type=jnp.float32).astype(jnp.bfloat16)
+
+
+def forward_kernel(coupling_ref, state_ref, table_ref, out_ref, turned):
+    step = pl.program_id(1)
+    levels, rows, lon = state_ref.shape
+    groups = levels * rows // LANES
+    initial = state_ref[...].astype(jnp.float32)
+    forcing = (initial + coupling_ref[...] * jnp.tanh(initial)).astype(jnp.bfloat16)
+    forcing = forcing.reshape(levels * rows, lon)
+    coeffs = lax.dot_general(
+        table_ref[...], forcing, (((1,), (1,)), ((), ())), preferred_element_type=jnp.float32
+    )
+    for group in range(groups):
+        turned[pl.ds(step * groups + group, coeffs.shape[0], stride=PACK), :] = coeffs[
+            :, group * LANES : (group + 1) * LANES
+        ]
+
+    @pl.when(step == pl.num_programs(1) - 1)
+    def _():
+        out_ref[...] = turned[...].reshape(out_ref.shape).astype(jnp.bfloat16)
+
+
+def forward_rows(state, table, coupling):
+    levels, rows, lon = state.shape
+    row_count = table.shape[0]
+    halves = levels * rows // (LANES * PACK)
+    step_levels = max(1, 256 // rows)
+    steps = levels // halves // step_levels
+    return pl.pallas_call(
+        forward_kernel,
+        grid=(halves, steps),
+        in_specs=[
+            pl.BlockSpec((1, rows, 1), lambda h, t: (0, 0, 0)),
+            pl.BlockSpec((step_levels, rows, lon), lambda h, t: (h * steps + t, 0, 0)),
+            pl.BlockSpec((row_count, lon), lambda h, t: (0, 0)),
+        ],
+        out_specs=pl.BlockSpec((row_count, PACK, LANES), lambda h, t: (0, h, 0)),
+        out_shape=jax.ShapeDtypeStruct((row_count, halves * PACK, LANES), jnp.bfloat16),
+        scratch_shapes=[pltpu.VMEM((row_count * PACK, LANES), jnp.float32)],
+        compiler_params=pltpu.CompilerParams(vmem_limit_bytes=VMEM),
+        cost_estimate=pl.CostEstimate(
+            flops=2 * levels * rows * lon * row_count,
+            bytes_accessed=2 * (state.size + table.size + row_count * levels * rows),
+            transcendentals=state.size,
+        ),
+    )(coupling, state, table)
+
+
+def spectral_kernel(rows, data_ref, table_ref, mask_ref, ratio_ref, eig_ref, in_ref, out_modes, out_ref):
+    waves, places, slots, lines, _ = data_ref.shape
+    parts = LANES // rows
+    modes = eig_ref.shape[0]
+    for slot in range(slots):
+        picked = []
+        for part in range(parts):
+            for place in range(places):
+                picked.append(
+                    jnp.concatenate(
+                        [
+                            data_ref[wave, place, slot][:, part * rows : (part + 1) * rows]
+                            for wave in range(waves)
+                        ],
+                        axis=1,
+                    )
+                )
+        table = table_ref[slot]
+        spectral = jnp.dot(
+            jnp.concatenate(picked, axis=0), table, preferred_element_type=jnp.float32
+        )
+        spectral = (spectral * mask_ref[slot]).astype(jnp.bfloat16)
+        modal = jnp.dot(in_ref[...], spectral, preferred_element_type=jnp.float32)
+        factor = 1.0 / (1.0 + eig_ref[...] * ratio_ref[slot])
+        modal = jnp.concatenate(
+            [modal[:modes] * factor, modal[modes:] * factor], axis=0
+        ).astype(jnp.bfloat16)
+        solved = jnp.dot(out_modes[...], modal, preferred_element_type=jnp.float32)
+        coeffs = lax.dot_general(
+            solved.astype(jnp.bfloat16),
+            table,
+            (((1,), (1,)), ((), ())),
+            preferred_element_type=jnp.float32,
+        ).astype(jnp.bfloat16)
+        for wave in range(waves):
+            for place in range(places):
+                out_ref[wave, place, slot] = jnp.concatenate(
+                    [
+                        coeffs[
+                            (part * places + place) * lines : (part * places + place + 1) * lines,
+                            wave * rows : (wave + 1) * rows,
+                        ]
+                        for part in range(parts)
+                    ],
+                    axis=1,
+                )
+
+
+def spectral_step(data, legendre, first, mask, ratio, eig_rates, inward, outward, rows):
+    waves, places, slots, lines, _ = data.shape
+    half_rows, half_count = legendre.shape[1:]
+    modes = eig_rates.shape[0]
+    block = math.gcd(slots, SLOTS_PER_STEP)
+    skip = first // block
+    whole = pl.BlockSpec(inward.shape, lambda i: (0, 0))
+    vector = pl.BlockSpec((block, 1, half_count), lambda i: (i + skip, 0, 0))
+    moved = pl.BlockSpec((waves, places, block, lines, LANES), lambda i: (0, 0, i, 0, 0))
+    return pl.pallas_call(
+        functools.partial(spectral_kernel, rows),
+        grid=(slots // block,),
+        in_specs=[
+            moved,
+            pl.BlockSpec((block, half_rows, half_count), lambda i: (i + skip, 0, 0)),
+            vector,
+            vector,
+            pl.BlockSpec((modes, 1), lambda i: (0, 0)),
+            whole,
+            whole,
+        ],
+        out_specs=moved,
+        out_shape=jax.ShapeDtypeStruct(data.shape, jnp.bfloat16),
+        compiler_params=pltpu.CompilerParams(vmem_limit_bytes=VMEM),
+        cost_estimate=pl.CostEstimate(
+            flops=8 * slots * half_rows * half_count * inward.shape[0],
+            bytes_accessed=2 * (2 * data.size + slots * half_rows * half_count),
+            transcendentals=0,
+        ),
+    )(data, legendre, mask, ratio, eig_rates.reshape(-1, 1), inward, outward)
+
+
+def inverse_kernel(chunks, sign_ref, *refs):
+    own_refs, other_refs = refs[:chunks], refs[chunks : 2 * chunks]
+    table_ref, out_ref, turned = refs[2 * chunks :]
+    step = pl.program_id(1)
+    levels, rows, lon = out_ref.shape
+    groups = levels * rows // LANES
+    blocks, chunk_rows = own_refs[0].shape[:2]
+
+    @pl.when(step == 0)
+    def _():
+        for block in range(blocks):
+            for chunk in range(chunks):
+                own = own_refs[chunk][block].astype(jnp.float32)
+                other = other_refs[chunk][block].astype(jnp.float32)
+                grid = (0.5 * (other + sign_ref[0] * own)).astype(jnp.bfloat16)
+                first = (block * chunks + chunk) * chunk_rows * PACK
+                turned[first : first + chunk_rows * PACK, :] = grid.astype(jnp.float32).reshape(
+                    -1, LANES
+                )
+
+    picked = jnp.concatenate(
+        [
+            turned[
+                pl.ds(step * groups + group, blocks * chunks * chunk_rows, stride=PACK), :
+            ].astype(jnp.bfloat16)
+            for group in range(groups)
+        ],
+        axis=1,
+    )
+    out = lax.dot_general(
+        picked, table_ref[...], (((0,), (0,)), ((), ())), preferred_element_type=jnp.float32
+    )
+    out_ref[...] = out.astype(jnp.bfloat16).reshape(out_ref.shape)
+
+
+def inverse_rows(own, other, table, sign, levels, rows):
+    chunks = len(own)
+    blocks, chunk_rows = own[0].shape[:2]
+    row_count, lon = table.shape
+    halves = levels * rows // (LANES * PACK)
+    step_levels = max(1, 256 // rows)
+    steps = levels // halves // step_levels
+    moved = pl.BlockSpec((blocks, chunk_rows, PACK, LANES), lambda h, t: (0, 0, h, 0))
+    return pl.pallas_call(
+        functools.partial(inverse_kernel, chunks),
+        grid=(halves, steps),
+        in_specs=[pl.BlockSpec(memory_space=pltpu.SMEM)]
+        + [moved] * (2 * chunks)
+        + [pl.BlockSpec((row_count, lon), lambda h, t: (0, 0))],
+        out_specs=pl.BlockSpec((step_levels, rows, lon), lambda h, t: (h * steps + t, 0, 0)),
+        out_shape=jax.ShapeDtypeStruct((levels, rows, lon), jnp.bfloat16),
+        scratch_shapes=[pltpu.VMEM((row_count * PACK, LANES), jnp.float32)],
+        compiler_params=pltpu.CompilerParams(vmem_limit_bytes=VMEM),
+        cost_estimate=pl.CostEstimate(
+            flops=2 * levels * rows * lon * row_count,
+            bytes_accessed=2 * (levels * rows * (lon + 2 * row_count) + table.size),
+            transcendentals=0,
+        ),
+    )(sign.reshape(1), *own, *other, table)
+
+
+def mode_maps(modes_in, modes_out, places, lines, parts):
+    modes, levels = modes_in.shape
+    groups = lines // 2
+    same = jnp.eye(2, dtype=modes_in.dtype)
+    inward = modes_in.reshape(modes, places, groups, parts)
+    inward = jnp.einsum("kvqb,cd->ckbvdq", inward, same).reshape(2 * modes, 2 * levels)
+    outward = modes_out.reshape(places, groups, parts, modes)
+    outward = jnp.einsum("vqbk,cd->bvdqck", outward, same).reshape(2 * levels, 2 * modes)
+    return inward, outward
+
+
+def aligned_shards(grid_state, legendre, wave_order, lat_order, eig_rates, modes_in, modes_out):
+    levels, _, rows, lon_count = grid_state.shape
+    wave_count = wave_order.shape[0]
+    half_rows = lat_order.shape[0]
+    half_count = legendre.shape[3]
+    slots = legendre.shape[0]
+    waves = lax.axis_size("wave")
+    places = lax.axis_size("level")
+    parity = lax.axis_index("fld")
+    wave_place = lax.axis_index("wave")
+    level_place = lax.axis_index("level")
+    owners = waves * places
+    lat_rows = lax.dynamic_slice_in_dim(lat_order, wave_place * rows, rows)
+    sine = jnp.sin((lat_rows.astype(jnp.float32) + 0.5) * (math.pi / (2.0 * half_rows)))
+    hemi_sign = 1.0 - 2.0 * parity.astype(jnp.float32)
+    coupling = (0.5 * hemi_sign * sine)[None, :, None]
+    table = selected_table(wave_order, lon_count)
+    own_waves = lax.dynamic_slice_in_dim(
+        wave_order, (wave_place * places + level_place) * slots, slots
+    )
+    mask = triangle_mask(own_waves, parity, half_count, wave_count)[:, None, :]
+    degree_f = degrees(own_waves, parity, half_count).astype(jnp.float32)
+    ratio = tau_scale * degree_f * (degree_f + 1.0) / float(wave_count * (wave_count - 1))
+    ratio = ratio[:, None, :]
+    parts = LANES // rows
+    groups = levels * rows // LANES
+    lines = 2 * groups
+    inward, outward = mode_maps(modes_in, modes_out, places, lines, parts)
+    state = grid_state.reshape(levels, rows, lon_count)
+    own_table = legendre.reshape(slots, half_rows, half_count)
+    chunks = math.gcd(SLOT_CHUNKS, slots)
+    chunk = slots // chunks
+    by_owner = table.reshape(owners, chunks, 2 * chunk, lon_count)
+    back_own, back_other = [], []
+    for part in range(chunks):
+        rows_here = forward_rows(state, by_owner[:, part].reshape(-1, lon_count), coupling)
+        mirror = partner(rows_here, "fld", 0)
+        mirrored = (
+            mirror.astype(jnp.float32) + hemi_sign * rows_here.astype(jnp.float32)
+        ).astype(jnp.bfloat16)
+        mirrored = mirrored.reshape(owners, chunk, lines, LANES)
+        data = lax.all_to_all(mirrored, ("wave", "level"), split_axis=0, concat_axis=0, tiled=True)
+        coeffs = spectral_step(
+            data.reshape(waves, places, chunk, lines, LANES),
+            own_table,
+            part * chunk,
+            mask,
+            ratio,
+            eig_rates,
+            inward,
+            outward,
+            rows,
+        )
+        back = lax.all_to_all(
+            coeffs.reshape(owners, chunk, lines, LANES),
+            ("wave", "level"),
+            split_axis=0,
+            concat_axis=0,
+            tiled=True,
+        ).reshape(owners, 2 * chunk, groups, LANES)
+        back_own.append(back)
+        back_other.append(partner(back, "fld", 0))
+    out = inverse_rows(back_own, back_other, table, hemi_sign, levels, rows)
+    return out.reshape(grid_state.shape)
+
+
+def shards(grid_state, legendre, *rest):
+    levels, _, rows, lon_count = grid_state.shape
+    aligned = (
+        rows % PACK == 0
+        and LANES % rows == 0
+        and (levels * rows) % (LANES * PACK) == 0
+        and levels % (max(1, 256 // rows) * (levels * rows // (LANES * PACK))) == 0
+        and lon_count % LANES == 0
+    )
+    run = aligned_shards if aligned else general_shards
+    return run(grid_state, legendre, *rest)
+
+
 def solution(mesh):
     placed = (
         P(("member", "level"), "fld", "wave", None),

time: 1010 us -> 527 us (0.52); the launches traced: 996 us -> 526 us
  local copies, waits for them, and re-layouts: 264 us -> 10.4 us
  blocking collectives: 291 us -> 187 us
  Pallas kernels: 0 us -> 98.1 us
  waiting for transfers between devices: 288 us -> 205 us
  matrix products: 77.3 us -> 6.87 us
  other arithmetic: 48.2 us -> 11.6 us
  between operations: 13.9 us -> 0.08 us
    all_to_all x2 -> x1, blocking collectives: 291 us -> 187 us  [aligned_shards(): lax.all_to_all(coeffs.reshape(owners, chunk, lines, LANES), ('wave', 'lev...]
    all_to_all x7 -> x0, local copies, waits for them, and re-layouts: 104 us -> none  [the longest x2 50.5 us: shards(): lax.all_to_all(mirrored, 'wave', split_axis=4, concat_axis=2, tiled=True)]
    pallas_call x0 -> x3, Pallas kernels: none -> 98.1 us  [the longest x1 37.1 us: spectral_step(): pl.pallas_call(functools.partial(spectral_kernel, rows), grid=(slots // b...]
    all_to_all x2 -> x1, waiting for transfers between devices: 261 us -> 178 us  [aligned_shards(): lax.all_to_all(mirrored, ('wave', 'level'), split_axis=0, concat_axis=0,...]
    convert_element_type x4 -> x0, local copies, waits for them, and re-layouts: 76.8 us -> none  [the longest x1 34.4 us: shards(): mirrored = (mirror_part.astype(jnp.float32) + hemi_sign * fourier_rows.as...]
    dot_general x5 -> x1, matrix products: 77.3 us -> 6.87 us  [selected_table(): jnp.dot(pick, rows, preferred_element_type=jnp.float32).astype(jnp.bfloat16)]
    another operation x2 -> x0, local copies, waits for them, and re-layouts: 26.6 us -> none
    unnamed x20 -> x13, local copies, waits for them, and re-layouts: 32.8 us -> 7.27 us
  transfers between devices with their start and end apart: 5 -> 3, of which waited for: 4 -> 3; matrix products, arithmetic and copies ran while one was open for 16% -> 1% of each run, Pallas kernels for 0% -> 0%
where the time goes in v1:
time: 527 us; the launch traced here: 526 us
  waiting for transfers between devices  205 us (39%)
  blocking collectives  187 us (35%)
  Pallas kernels  98.1 us (19%)
  other arithmetic  11.6 us (2%)
  local copies, waits for them, and re-layouts  10.4 us (2%)
  starting transfers between devices  7.77 us (1%)
  matrix products  6.87 us (1%)
    all_to_all x1, blocking collectives, aligned_shards(): lax.all_to_all(coeffs.reshape(owners, chunk, lines, LANES), ('wave', 'lev...  187 us
    all_to_all x1, waiting for transfers between devices, aligned_shards(): lax.all_to_all(mirrored, ('wave', 'level'), split_axis=0, concat_axis=0,...  178 us
    pallas_call x1, Pallas kernels, spectral_step(): pl.pallas_call(functools.partial(spectral_kernel, rows), grid=(slots // b...  37.1 us
    pallas_call x1, Pallas kernels, inverse_rows(): pl.pallas_call(functools.partial(inverse_kernel, chunks), grid=(halves, s...  34.1 us
    pallas_call x1, Pallas kernels, forward_rows(): pl.pallas_call(forward_kernel, grid=(halves, steps), in_specs=[pl.BlockSp...  26.9 us
    ppermute x2, waiting for transfers between devices, partner(): return lax.ppermute(value, axis, pairs)  26.2 us
  transfers between devices with their start and end apart: 3, of which 3 were waited for; matrix products, arithmetic and copies ran while one was open for 1% of the time, Pallas kernels for 0%

profile of v1, /device:TPU:0, one launch (start us, length us, event | category | flops | bytes accessed | tf_op | source)
XLA Modules:
  0.0 526.3 jit_solution(1531296855728820485)
XLA Ops:
  0.0 0.7 broadcast_multiply_fusion.2
  0.7 0.8 multiply_bitcast_fusion
  1.5 0.7 copy.22.coupling_ref
  2.2 0.1 iota_add_fusion
  2.3 0.2 add.107
  2.5 6.9 %fusion.1.table_ref.refs_2_ = bf16[1024,1536]{1,0:T(8,128)(2,1)} fusion(bf16[1024,1536]{1,0:T(8,128)(2,1)} %constant.41.clone, s32[1024]{0:T(1024)S(1)} %add.107), kind=kOutput, calls=%fused_computation.3 | convolution fusion | flops 3223846912 | bytes 6295552 | tf_op jit(solution)/shard_map/dot_general | solution.py:137
  9.4 26.9 %shard_map.82 = bf16[1024,32,128]{2,1,0:T(8,128)(2,1)} custom-call(f32[1,64,1]{2,1,0:T(8,128)} %copy.22.coupling_ref, bf16[64,64,1536]{2,1,0:T(8,128)(2,1)} %bitcast.41, bf16[1024,1536]{1,0:T(8,128)(2,1)} %fusion.1.table_ref.refs_2_), custom_call_target="tpu_custom_call" | custom-call | flops 12884901888 | bytes 24117248 | tf_op jit(solution)/shard_map/pallas_call | solution.py:166
  36.3 0.4 collective-permute-start
  36.7 13.0 %collective-permute-done = bf16[1024,32,128]{2,1,0:T(8,128)(2,1)S(1)} collective-permute-done((bf16[1024,32,128]{2,1,0:T(8,128)(2,1)}, bf16[1024,32,128]{2,1,0:T(8,128)(2,1)S(1)}, u32[]{:S(2)}, u32[]{:S(2)}) %collective-permute-start) | collective-permute-done | bytes 8388640 | tf_op jit(solution)/shard_map/ppermute | solution.py:24
  49.7 8.1 %add_convert_fusion = bf16[1024,32,128]{2,1,0:T(8,128)(2,1)} fusion(bf16[1024,32,128]{2,1,0:T(8,128)(2,1)} %shard_map.82, bf16[1024,32,128]{2,1,0:T(8,128)(2,1)S(1)} %collective-permute-done, f32[]{:T(128)} %sub.3), kind=kLoop, calls=%fused_computation | loop fusion | flops 20971520 | bytes 25165828 | tf_op jit(solution)/shard_map/convert_element_type | solution.py:377
  57.8 0.0 copy-start.1
  57.8 0.0 copy-start.2
  57.8 0.0 copy-start.3
  57.8 7.3 %all-to-all-start = ((bf16[8,64,64,128]{3,2,1,0:T(8,128)(2,1)}), bf16[8,64,64,128]{3,2,1,0:T(8,128)(2,1)}, u32[]{:S(2)}, u32[]{:S(2)}) async-start(bf16[8,64,64,128]{3,2,1,0:T(8,128)(2,1)} %bitcast.30), calls=%async_computation | async-start | bytes 16777216 | tf_op jit(solution)/shard_map/all_to_all | solution.py:379
  65.1 0.8 dynamic_slice.7
  65.9 0.0 copy-done.1
  65.9 0.1 copy.24
  66.0 0.0 copy-done.2
  66.0 0.0 copy-done.3
  66.0 0.7 copy.27.eig_ref
  66.8 0.2 broadcast_multiply_fusion
  67.0 0.7 copy.34
  67.6 0.2 broadcast_multiply_fusion.1
  67.8 0.8 copy.28.in_ref
  68.6 0.8 multiply_multiply_fusion.ratio_ref
  69.4 0.8 compare_convert_fusion.mask_ref
  70.2 178.4 %all-to-all-done = bf16[8,64,64,128]{3,2,1,0:T(8,128)(2,1)} async-done(((bf16[8,64,64,128]{3,2,1,0:T(8,128)(2,1)}), bf16[8,64,64,128]{3,2,1,0:T(8,128)(2,1)}, u32[]{:S(2)}, u32[]{:S(2)}) %all-to-all-start) | async-done | bytes 8388640 | tf_op jit(solution)/shard_map/all_to_all | solution.py:379
  248.6 37.1 %shard_map.83 = bf16[4,2,64,64,128]{4,3,2,1,0:T(8,128)(2,1)} custom-call(bf16[4,2,64,64,128]{4,3,2,1,0:T(8,128)(2,1)} %bitcast.4.data_ref, bf16[64,256,256]{2,1,0:T(8,128)(2,1)} %bitcast.42, f32[64,1,256]{2,1,0:T(1,128)} %compare_convert_fusion.mask_ref, f32[64,1,256]{2,1,0:T(1,128)} %multiply_multiply_fusion.ratio_ref, f32[128,1]{1,0:T(8,128)} %copy.27.eig_ref, ...), custom_call_target="tpu_custom_call" | custom-call | flops 8589934592 | bytes 25165824 | tf_op jit(solution)/shard_map/pallas_call | solution.py:243
  285.7 186.9 %all_to_all.10 = bf16[8,64,64,128]{3,2,1,0:T(8,128)(2,1)S(1)} all-to-all(bf16[8,64,64,128]{3,2,1,0:T(8,128)(2,1)} %bitcast.33), channel_id=1, replica_groups=mesh['member'=2,'wave'=4,'level'=2,'fld'=2] {'wave','level'}, dimensions={0} | all-to-all | bytes 16777216 | tf_op jit(solution)/shard_map/all_to_all | solution.py:391
  472.5 0.0 copy-start
  472.5 3.2 copy-done
  475.8 0.0 collective-permute-start.1
  475.8 13.2 %collective-permute-done.1.refs_1_ = bf16[8,128,32,128]{3,2,1,0:T(8,128)(2,1)S(1)} collective-permute-done((bf16[8,128,32,128]{3,2,1,0:T(8,128)(2,1)S(1)}, bf16[8,128,32,128]{3,2,1,0:T(8,128)(2,1)S(1)}, u32[]{:S(2)}, u32[]{:S(2)}) %collective-permute-start.1) | collective-permute-done | bytes 8388640 | tf_op jit(solution)/shard_map/ppermute | solution.py:24
  488.9 0.0 copy-start.4
  488.9 3.2 copy-done.4
  492.2 34.1 %shard_map.84 = bf16[64,64,1536]{2,1,0:T(8,128)(2,1)} custom-call(f32[1]{0:T(128)} %bitcast.sign_ref, bf16[8,128,32,128]{3,2,1,0:T(8,128)(2,1)} %bitcast.32, bf16[8,128,32,128]{3,2,1,0:T(8,128)(2,1)} %copy-done.4, bf16[1024,1536]{1,0:T(8,128)(2,1)} %fusion.1.table_ref.refs_2_), custom_call_target="tpu_custom_call" | custom-call | flops 12884901888 | bytes 32505856 | tf_op jit(solution)/shard_map/pallas_call | solution.py:309
  (5 shorter events, 0.0 us)
Async XLA Ops:
  36.3 13.4 %collective-permute-start = (bf16[1024,32,128]{2,1,0:T(8,128)(2,1)}, bf16[1024,32,128]{2,1,0:T(8,128)(2,1)S(1)}, u32[]{:S(2)}, u32[]{:S(2)}) collective-permute-start(bf16[1024,32,128]{2,1,0:T(8,128)(2,1)} %shard_map.82), channel_id=1, source_target_pairs={{0,1},{1,0},{2,3},{3,2},{4,5},{5,4},{6,7},{7,6},{8,9},{9,8},{10,11... | collective-permute-start | bytes 25165832 | tf_op jit(solution)/shard_map/ppermute | solution.py:24
  57.8 8.1 %copy-start.1 = (bf16[128,128]{1,0:T(8,128)(2,1)S(1)}, bf16[128,128]{1,0:T(8,128)(2,1)}, u32[]{:S(2)}) copy-start(bf16[128,128]{1,0:T(8,128)(2,1)} %param.13) | copy-start | bytes 98308
  57.8 8.2 %copy-start.2 = (bf16[128,128]{1,0:T(8,128)(2,1)S(1)}, bf16[128,128]{1,0:T(8,128)(2,1)}, u32[]{:S(2)}) copy-start(bf16[128,128]{1,0:T(8,128)(2,1)} %param.14) | copy-start | bytes 98308
  57.8 8.2 %copy-start.3 = (f32[128]{0:T(128)S(1)}, f32[128]{0:T(128)}, u32[]{:S(2)}) copy-start(f32[128]{0:T(128)} %param.12) | copy-start | bytes 1540
  57.8 190.8 %all-to-all-start = ((bf16[8,64,64,128]{3,2,1,0:T(8,128)(2,1)}), bf16[8,64,64,128]{3,2,1,0:T(8,128)(2,1)}, u32[]{:S(2)}, u32[]{:S(2)}) async-start(bf16[8,64,64,128]{3,2,1,0:T(8,128)(2,1)} %bitcast.30), calls=%async_computation | async-start | bytes 16777216 | tf_op jit(solution)/shard_map/all_to_all | solution.py:379
  472.5 3.2 copy-start
  475.8 13.2 %collective-permute-start.1 = (bf16[8,128,32,128]{3,2,1,0:T(8,128)(2,1)S(1)}, bf16[8,128,32,128]{3,2,1,0:T(8,128)(2,1)S(1)}, u32[]{:S(2)}, u32[]{:S(2)}) collective-permute-start(bf16[8,128,32,128]{3,2,1,0:T(8,128)(2,1)S(1)} %bitcast.31), channel_id=1, source_target_pairs={{0,1},{1,0},{2,3},{3,2},{4,5},{5,4},{6,7},{7,6},{8,9},{9,8},{10,11... | collective-permute-start | bytes 25165832 | tf_op jit(solution)/shard_map/ppermute | solution.py:24
  488.9 3.2 copy-start.4

commit v2 on v1

--- a/solution.py
+++ b/solution.py
@@ -11,7 +11,7 @@
 
 LANES = 128
 PACK = 16
-SLOT_CHUNKS = 1
+SLOT_CHUNKS = 2
 SLOTS_PER_STEP = 4
 VMEM = 60 * 1024 * 1024
 
@@ -125,8 +125,7 @@
     return current
 
 
-def selected_table(wave_order, lon_count):
-    wave_count = wave_order.shape[0]
+def selected_table(wave_order, wave_count, lon_count):
     phase = np.arange(wave_count)[:, None] * np.arange(lon_count)[None, :] % lon_count
     angles = phase * (2.0 * math.pi / lon_count)
     rows = np.stack([np.cos(angles), -np.sin(angles)], axis=1) * math.sqrt(2.0 / lon_count)
@@ -161,7 +160,7 @@
     levels, rows, lon = state.shape
     row_count = table.shape[0]
     halves = levels * rows // (LANES * PACK)
-    step_levels = max(1, 256 // rows)
+    step_levels = max(1, 512 // rows)
     steps = levels // halves // step_levels
     return pl.pallas_call(
         forward_kernel,
@@ -263,65 +262,77 @@
     )(data, legendre, mask, ratio, eig_rates.reshape(-1, 1), inward, outward)
 
 
-def inverse_kernel(chunks, sign_ref, *refs):
-    own_refs, other_refs = refs[:chunks], refs[chunks : 2 * chunks]
-    table_ref, out_ref, turned = refs[2 * chunks :]
+def inverse_kernel(sign_ref, own_ref, other_ref, table_ref, *refs):
+    sum_refs, (out_ref, turned) = refs[:-2], refs[-2:]
     step = pl.program_id(1)
     levels, rows, lon = out_ref.shape
     groups = levels * rows // LANES
-    blocks, chunk_rows = own_refs[0].shape[:2]
+    row_count = own_ref.shape[0]
 
     @pl.when(step == 0)
     def _():
-        for block in range(blocks):
-            for chunk in range(chunks):
-                own = own_refs[chunk][block].astype(jnp.float32)
-                other = other_refs[chunk][block].astype(jnp.float32)
-                grid = (0.5 * (other + sign_ref[0] * own)).astype(jnp.bfloat16)
-                first = (block * chunks + chunk) * chunk_rows * PACK
-                turned[first : first + chunk_rows * PACK, :] = grid.astype(jnp.float32).reshape(
-                    -1, LANES
-                )
+        own = own_ref[...].astype(jnp.float32)
+        other = other_ref[...].astype(jnp.float32)
+        grid = (0.5 * (other + sign_ref[0] * own)).astype(jnp.bfloat16)
+        turned[...] = grid.astype(jnp.float32).reshape(-1, LANES)
 
     picked = jnp.concatenate(
         [
-            turned[
-                pl.ds(step * groups + group, blocks * chunks * chunk_rows, stride=PACK), :
-            ].astype(jnp.bfloat16)
+            turned[pl.ds(step * groups + group, row_count, stride=PACK), :].astype(jnp.bfloat16)
             for group in range(groups)
         ],
         axis=1,
     )
     out = lax.dot_general(
         picked, table_ref[...], (((0,), (0,)), ((), ())), preferred_element_type=jnp.float32
-    )
-    out_ref[...] = out.astype(jnp.bfloat16).reshape(out_ref.shape)
-
-
-def inverse_rows(own, other, table, sign, levels, rows):
-    chunks = len(own)
-    blocks, chunk_rows = own[0].shape[:2]
+    ).reshape(out_ref.shape)
+    for sum_ref in sum_refs:
+        out = out + sum_ref[...]
+    out_ref[...] = out.astype(out_ref.dtype)
+
+
+def inverse_rows(own, other, table, sign, so_far, levels, rows, dtype):
     row_count, lon = table.shape
     halves = levels * rows // (LANES * PACK)
-    step_levels = max(1, 256 // rows)
+    step_levels = max(1, 512 // rows)
     steps = levels // halves // step_levels
-    moved = pl.BlockSpec((blocks, chunk_rows, PACK, LANES), lambda h, t: (0, 0, h, 0))
+    moved = pl.BlockSpec((row_count, PACK, LANES), lambda h, t: (0, h, 0))
+    result = pl.BlockSpec((step_levels, rows, lon), lambda h, t: (h * steps + t, 0, 0))
     return pl.pallas_call(
-        functools.partial(inverse_kernel, chunks),
+        inverse_kernel,
         grid=(halves, steps),
-        in_specs=[pl.BlockSpec(memory_space=pltpu.SMEM)]
-        + [moved] * (2 * chunks)
-        + [pl.BlockSpec((row_count, lon), lambda h, t: (0, 0))],
-        out_specs=pl.BlockSpec((step_levels, rows, lon), lambda h, t: (h * steps + t, 0, 0)),
-        out_shape=jax.ShapeDtypeStruct((levels, rows, lon), jnp.bfloat16),
+        in_specs=[
+            pl.BlockSpec(memory_space=pltpu.SMEM),
+            moved,
+            moved,
+            pl.BlockSpec((row_count, lon), lambda h, t: (0, 0)),
+        ]
+        + [result] * len(so_far),
+        out_specs=result,
+        out_shape=jax.ShapeDtypeStruct((levels, rows, lon), dtype),
         scratch_shapes=[pltpu.VMEM((row_count * PACK, LANES), jnp.float32)],
         compiler_params=pltpu.CompilerParams(vmem_limit_bytes=VMEM),
         cost_estimate=pl.CostEstimate(
             flops=2 * levels * rows * lon * row_count,
-            bytes_accessed=2 * (levels * rows * (lon + 2 * row_count) + table.size),
+            bytes_accessed=2 * (levels * rows * (3 * lon + 2 * row_count) + table.size),
             transcendentals=0,
         ),
-    )(sign.reshape(1), *own, *other, table)
+    )(sign.reshape(1), own, other, table, *so_far)
+
+
+def untouched(*refs):
+    del refs
+
+
+def after(value, done):
+    anywhere = pl.BlockSpec(memory_space=pl.ANY)
+    return pl.pallas_call(
+        untouched,
+        in_specs=[anywhere] * (1 + len(done)),
+        out_specs=anywhere,
+        out_shape=jax.ShapeDtypeStruct(value.shape, value.dtype),
+        input_output_aliases={0: 0},
+    )(value, *done)
 
 
 def mode_maps(modes_in, modes_out, places, lines, parts):
@@ -351,7 +362,6 @@
     sine = jnp.sin((lat_rows.astype(jnp.float32) + 0.5) * (math.pi / (2.0 * half_rows)))
     hemi_sign = 1.0 - 2.0 * parity.astype(jnp.float32)
     coupling = (0.5 * hemi_sign * sine)[None, :, None]
-    table = selected_table(wave_order, lon_count)
     own_waves = lax.dynamic_slice_in_dim(
         wave_order, (wave_place * places + level_place) * slots, slots
     )
@@ -367,10 +377,11 @@
     own_table = legendre.reshape(slots, half_rows, half_count)
     chunks = math.gcd(SLOT_CHUNKS, slots)
     chunk = slots // chunks
-    by_owner = table.reshape(owners, chunks, 2 * chunk, lon_count)
-    back_own, back_other = [], []
+    by_owner = wave_order.reshape(owners, chunks, chunk)
+    tables, backs = [], []
     for part in range(chunks):
-        rows_here = forward_rows(state, by_owner[:, part].reshape(-1, lon_count), coupling)
+        table = selected_table(by_owner[:, part].reshape(-1), wave_count, lon_count)
+        rows_here = forward_rows(state, table, coupling)
         mirror = partner(rows_here, "fld", 0)
         mirrored = (
             mirror.astype(jnp.float32) + hemi_sign * rows_here.astype(jnp.float32)
@@ -394,10 +405,16 @@
             split_axis=0,
             concat_axis=0,
             tiled=True,
-        ).reshape(owners, 2 * chunk, groups, LANES)
-        back_own.append(back)
-        back_other.append(partner(back, "fld", 0))
-    out = inverse_rows(back_own, back_other, table, hemi_sign, levels, rows)
+        ).reshape(owners * 2 * chunk, groups, LANES)
+        tables.append(table)
+        backs.append(back)
+    so_far = []
+    for part in range(chunks):
+        dtype = jnp.bfloat16 if part == chunks - 1 else jnp.bfloat16
+        own = after(backs[part], so_far) if so_far else backs[part]
+        other = partner(own, "fld", 0)
+        out = inverse_rows(own, other, tables[part], hemi_sign, so_far, levels, rows, dtype)
+        so_far = [out]
     return out.reshape(grid_state.shape)
 
 
@@ -407,7 +424,7 @@
         rows % PACK == 0
         and LANES % rows == 0
         and (levels * rows) % (LANES * PACK) == 0
-        and levels % (max(1, 256 // rows) * (levels * rows // (LANES * PACK))) == 0
+        and levels % (max(1, 512 // rows) * (levels * rows // (LANES * PACK))) == 0
         and lon_count % LANES == 0
     )
     run = aligned_shards if aligned else general_shards

time: 527 us -> 458 us (0.87)
  blocking collectives: 187 us -> 0 us
  waiting for transfers between devices: 205 us -> 298 us
  starting transfers between devices: 7.77 us -> 22 us
  Pallas kernels: 98.1 us -> 109 us
  local copies, waits for them, and re-layouts: 10.4 us -> 4.95 us
    all_to_all x1 -> x0, blocking collectives: 187 us -> none  [aligned_shards(): lax.all_to_all(coeffs.reshape(owners, chunk, lines, LANES), ('wave', 'lev...]
    all_to_all x0 -> x2, waiting for transfers between devices: none -> 139 us  [aligned_shards(): lax.all_to_all(coeffs.reshape(owners, chunk, lines, LANES), ('wave', 'lev...]
    all_to_all x1 -> x2, waiting for transfers between devices: 178 us -> 130 us  [aligned_shards(): lax.all_to_all(mirrored, ('wave', 'level'), split_axis=0, concat_axis=0,...]
    all_to_all x0 -> x2, starting transfers between devices: none -> 9.13 us  [aligned_shards(): lax.all_to_all(coeffs.reshape(owners, chunk, lines, LANES), ('wave', 'lev...]
    unnamed x13 -> x11, local copies, waits for them, and re-layouts: 7.27 us -> 0.81 us
    pallas_call x1 -> x3, Pallas kernels: 34.1 us -> 39.5 us  [the longest x2 39.5 us: inverse_rows(): pl.pallas_call(inverse_kernel, grid=(halves, steps), in_specs=[pl.BlockSp...]
    all_to_all x1 -> x2, starting transfers between devices: 7.32 us -> 12.3 us  [aligned_shards(): lax.all_to_all(mirrored, ('wave', 'level'), split_axis=0, concat_axis=0,...]
    pallas_call x1 -> x2, Pallas kernels: 26.9 us -> 30.6 us  [forward_rows(): pl.pallas_call(forward_kernel, grid=(halves, steps), in_specs=[pl.BlockSp...]
  transfers between devices with their start and end apart: 3 -> 8, of which waited for: 3 -> 8; matrix products, arithmetic and copies ran while one was open for 1% -> 3% of each run, Pallas kernels for 0% -> 16%
where the time goes in v2:
time: 458 us; the launch traced here: 457 us
  waiting for transfers between devices  298 us (65%)
  Pallas kernels  109 us (24%)
  starting transfers between devices  22 us (5%)
  other arithmetic  14 us (3%)
  matrix products  7.9 us (2%)
  local copies, waits for them, and re-layouts  4.95 us (1%)
    all_to_all x2, waiting for transfers between devices, aligned_shards(): lax.all_to_all(coeffs.reshape(owners, chunk, lines, LANES), ('wave', 'lev...  139 us
    all_to_all x2, waiting for transfers between devices, aligned_shards(): lax.all_to_all(mirrored, ('wave', 'level'), split_axis=0, concat_axis=0,...  130 us
    pallas_call x2, Pallas kernels, inverse_rows(): pl.pallas_call(inverse_kernel, grid=(halves, steps), in_specs=[pl.BlockSp...  39.5 us
    pallas_call x2, Pallas kernels, spectral_step(): pl.pallas_call(functools.partial(spectral_kernel, rows), grid=(slots // b...  39.2 us
    pallas_call x2, Pallas kernels, forward_rows(): pl.pallas_call(forward_kernel, grid=(halves, steps), in_specs=[pl.BlockSp...  30.6 us
    ppermute x4, waiting for transfers between devices, partner(): return lax.ppermute(value, axis, pairs)  29.3 us
    all_to_all x2, starting transfers between devices, aligned_shards(): lax.all_to_all(mirrored, ('wave', 'level'), split_axis=0, concat_axis=0,...  12.3 us
    convert_element_type x2, other arithmetic, aligned_shards(): mirrored = (mirror.astype(jnp.float32) + hemi_sign * rows_here.astype(jnp...  11.1 us
  transfers between devices with their start and end apart: 8, of which 8 were waited for; matrix products, arithmetic and copies ran while one was open for 3% of the time, Pallas kernels for 16%

profile of v2, /device:TPU:0, one launch (start us, length us, event | category | flops | bytes accessed | tf_op | source)
XLA Modules:
  0.0 456.6 jit_solution(9665644637875085839)
XLA Ops:
  0.0 0.8 reshape.208
  0.8 0.1 mul.109
  0.9 0.8 multiply_bitcast_fusion
  1.7 0.7 copy.29.coupling_ref
  2.4 0.1 iota_add_fusion
  2.5 0.1 add.144
  2.6 4.9 %convolution_convert_fusion.table_ref = bf16[512,1536]{1,0:T(8,128)(2,1)} fusion(bf16[1024,1536]{1,0:T(8,128)(2,1)} %constant.41.clone, s32[512]{0:T(512)S(1)} %add.144), kind=kOutput, calls=%fused_computation.2 | convolution fusion | flops 1611923456 | bytes 4720640 | tf_op jit(solution)/shard_map/dot_general | solution.py:136
  7.5 15.3 %shard_map.93 = bf16[512,32,128]{2,1,0:T(8,128)(2,1)} custom-call(f32[1,64,1]{2,1,0:T(8,128)} %copy.29.coupling_ref, bf16[64,64,1536]{2,1,0:T(8,128)(2,1)} %bitcast.49, bf16[512,1536]{1,0:T(8,128)(2,1)} %convolution_convert_fusion.table_ref), custom_call_target="tpu_custom_call" | custom-call | flops 6442450944 | bytes 18350080 | tf_op jit(solution)/shard_map/pallas_call | solution.py:165
  22.8 0.5 collective-permute-start.1
  23.3 7.0 %collective-permute-done.1 = bf16[512,32,128]{2,1,0:T(8,128)(2,1)S(1)} collective-permute-done((bf16[512,32,128]{2,1,0:T(8,128)(2,1)}, bf16[512,32,128]{2,1,0:T(8,128)(2,1)S(1)}, u32[]{:S(2)}, u32[]{:S(2)}) %collective-permute-start.1) | collective-permute-done | bytes 4194336 | tf_op jit(solution)/shard_map/ppermute | solution.py:24
  30.3 5.5 %add_convert_fusion = bf16[512,32,128]{2,1,0:T(8,128)(2,1)} fusion(bf16[512,32,128]{2,1,0:T(8,128)(2,1)} %shard_map.93, bf16[512,32,128]{2,1,0:T(8,128)(2,1)S(1)} %collective-permute-done.1, f32[]{:T(128)} %sub.3), kind=kLoop, calls=%fused_computation | loop fusion | flops 10485760 | bytes 12582916 | tf_op jit(solution)/shard_map/convert_element_type | solution.py:388
  35.8 0.0 copy-start.3
  35.8 7.4 %all-to-all-start.2 = ((bf16[8,32,64,128]{3,2,1,0:T(8,128)(2,1)}), bf16[8,32,64,128]{3,2,1,0:T(8,128)(2,1)}, u32[]{:S(2)}, u32[]{:S(2)}) async-start(bf16[8,32,64,128]{3,2,1,0:T(8,128)(2,1)} %bitcast.38), calls=%async_computation.2 | async-start | bytes 8388608 | tf_op jit(solution)/shard_map/all_to_all | solution.py:390
  43.2 0.1 mul.99
  43.2 0.1 iota_add_fusion.1
  43.3 0.1 add.130
  43.5 0.0 copy-done.3
  43.5 3.0 convolution_convert_fusion.1.table_ref
  46.5 15.3 %shard_map.91 = bf16[512,32,128]{2,1,0:T(8,128)(2,1)} custom-call(f32[1,64,1]{2,1,0:T(8,128)} %copy.29.coupling_ref, bf16[64,64,1536]{2,1,0:T(8,128)(2,1)} %bitcast.50, bf16[512,1536]{1,0:T(8,128)(2,1)} %convolution_convert_fusion.1.table_ref), custom_call_target="tpu_custom_call" | custom-call | flops 6442450944 | bytes 18350080 | tf_op jit(solution)/shard_map/pallas_call | solution.py:165
  61.8 0.0 collective-permute-start
  61.8 7.4 %collective-permute-done = bf16[512,32,128]{2,1,0:T(8,128)(2,1)S(1)} collective-permute-done((bf16[512,32,128]{2,1,0:T(8,128)(2,1)}, bf16[512,32,128]{2,1,0:T(8,128)(2,1)S(1)}, u32[]{:S(2)}, u32[]{:S(2)}) %collective-permute-start) | collective-permute-done | bytes 4194336 | tf_op jit(solution)/shard_map/ppermute | solution.py:24
  69.2 5.6 %add_convert_fusion.1 = bf16[512,32,128]{2,1,0:T(8,128)(2,1)} fusion(bf16[512,32,128]{2,1,0:T(8,128)(2,1)} %shard_map.91, bf16[512,32,128]{2,1,0:T(8,128)(2,1)S(1)} %collective-permute-done, f32[]{:T(128)} %sub.3), kind=kLoop, calls=%fused_computation.1 | loop fusion | flops 10485760 | bytes 12582916 | tf_op jit(solution)/shard_map/convert_element_type | solution.py:388
  74.7 62.0 %all-to-all-done.2 = bf16[8,32,64,128]{3,2,1,0:T(8,128)(2,1)} async-done(((bf16[8,32,64,128]{3,2,1,0:T(8,128)(2,1)}), bf16[8,32,64,128]{3,2,1,0:T(8,128)(2,1)}, u32[]{:S(2)}, u32[]{:S(2)}) %all-to-all-start.2) | async-done | bytes 4194336 | tf_op jit(solution)/shard_map/all_to_all | solution.py:390
  136.7 0.0 copy-start
  136.7 0.0 copy-start.1
  136.7 0.0 copy-start.2
  136.7 4.9 %all-to-all-start = ((bf16[8,32,64,128]{3,2,1,0:T(8,128)(2,1)}), bf16[8,32,64,128]{3,2,1,0:T(8,128)(2,1)}, u32[]{:S(2)}, u32[]{:S(2)}) async-start(bf16[8,32,64,128]{3,2,1,0:T(8,128)(2,1)} %bitcast.37), calls=%async_computation | async-start | bytes 8388608 | tf_op jit(solution)/shard_map/all_to_all | solution.py:390
  141.6 0.8 dynamic_slice.7
  142.4 0.0 copy-done
  142.4 0.1 copy.31
  142.5 0.0 copy-done.1
  142.6 0.0 copy-done.2
  142.6 0.7 copy.34.eig_ref
  143.3 0.2 broadcast_multiply_fusion
  143.5 0.7 copy.44
  144.1 0.2 broadcast_multiply_fusion.1
  144.3 0.7 copy.35.in_ref
  145.1 0.8 multiply_multiply_fusion.ratio_ref
  145.9 0.8 compare_convert_fusion.mask_ref
  146.6 19.6 %shard_map.94 = bf16[4,2,32,64,128]{4,3,2,1,0:T(8,128)(2,1)} custom-call(bf16[4,2,32,64,128]{4,3,2,1,0:T(8,128)(2,1)} %bitcast.14.data_ref, bf16[64,256,256]{2,1,0:T(8,128)(2,1)} %bitcast.35, f32[64,1,256]{2,1,0:T(1,128)} %compare_convert_fusion.mask_ref, f32[64,1,256]{2,1,0:T(1,128)} %multiply_multiply_fusion.ratio_ref, f32[128,1]{1,0:T(8,128)} %copy.34.eig_ref, ...), custom_call_target="tpu_custom_call" | custom-call | flops 4294967296 | bytes 12582912 | tf_op jit(solution)/shard_map/pallas_call | solution.py:242
  166.2 67.9 %all-to-all-done = bf16[8,32,64,128]{3,2,1,0:T(8,128)(2,1)} async-done(((bf16[8,32,64,128]{3,2,1,0:T(8,128)(2,1)}), bf16[8,32,64,128]{3,2,1,0:T(8,128)(2,1)}, u32[]{:S(2)}, u32[]{:S(2)}) %all-to-all-start) | async-done | bytes 4194336 | tf_op jit(solution)/shard_map/all_to_all | solution.py:390
  234.1 4.6 %all-to-all-start.3 = ((bf16[8,32,64,128]{3,2,1,0:T(8,128)(2,1)}), bf16[8,32,64,128]{3,2,1,0:T(8,128)(2,1)}, u32[]{:S(2)}, u32[]{:S(2)}) async-start(bf16[8,32,64,128]{3,2,1,0:T(8,128)(2,1)} %bitcast.40), calls=%async_computation.3 | async-start | bytes 8388608 | tf_op jit(solution)/shard_map/all_to_all | solution.py:402
  238.7 19.7 %shard_map.92 = bf16[4,2,32,64,128]{4,3,2,1,0:T(8,128)(2,1)} custom-call(bf16[4,2,32,64,128]{4,3,2,1,0:T(8,128)(2,1)} %bitcast.4.data_ref, bf16[64,256,256]{2,1,0:T(8,128)(2,1)} %bitcast.36, f32[64,1,256]{2,1,0:T(1,128)} %compare_convert_fusion.mask_ref, f32[64,1,256]{2,1,0:T(1,128)} %multiply_multiply_fusion.ratio_ref, f32[128,1]{1,0:T(8,128)} %copy.34.eig_ref, ...), custom_call_target="tpu_custom_call" | custom-call | flops 4294967296 | bytes 12582912 | tf_op jit(solution)/shard_map/pallas_call | solution.py:242
  258.3 72.9 %all-to-all-done.3 = bf16[8,32,64,128]{3,2,1,0:T(8,128)(2,1)} async-done(((bf16[8,32,64,128]{3,2,1,0:T(8,128)(2,1)}), bf16[8,32,64,128]{3,2,1,0:T(8,128)(2,1)}, u32[]{:S(2)}, u32[]{:S(2)}) %all-to-all-start.3) | async-done | bytes 4194336 | tf_op jit(solution)/shard_map/all_to_all | solution.py:402
  331.2 4.6 all-to-all-start.1
  335.8 0.1 collective-permute-start.2
  335.8 7.5 %collective-permute-done.2.other_ref = bf16[512,32,128]{2,1,0:T(8,128)(2,1)} collective-permute-done((bf16[512,32,128]{2,1,0:T(8,128)(2,1)}, bf16[512,32,128]{2,1,0:T(8,128)(2,1)}, u32[]{:S(2)}, u32[]{:S(2)}) %collective-permute-start.2) | collective-permute-done | bytes 4194336 | tf_op jit(solution)/shard_map/ppermute | solution.py:24
  343.3 18.7 %shard_map.95.refs_1_.refs_0_ = bf16[64,64,1536]{2,1,0:T(8,128)(2,1)} custom-call(f32[1]{0:T(128)} %bitcast.sign_ref, bf16[512,32,128]{2,1,0:T(8,128)(2,1)} %bitcast.16.own_ref, bf16[512,32,128]{2,1,0:T(8,128)(2,1)} %collective-permute-done.2.other_ref, bf16[512,1536]{1,0:T(8,128)(2,1)} %convolution_convert_fusion.table_ref), custom_call_target="tpu_custom_call" | custom-call | flops 6442450944 | bytes 47710208 | tf_op jit(solution)/shard_map/pallas_call | solution.py:301
  362.0 66.3 %all-to-all-done.1 = bf16[8,32,64,128]{3,2,1,0:T(8,128)(2,1)} async-done(((bf16[8,32,64,128]{3,2,1,0:T(8,128)(2,1)}), bf16[8,32,64,128]{3,2,1,0:T(8,128)(2,1)}, u32[]{:S(2)}, u32[]{:S(2)}) %all-to-all-start.1) | async-done | bytes 4194336 | tf_op jit(solution)/shard_map/all_to_all | solution.py:402
  428.3 0.0 collective-permute-start.3
  428.3 7.5 %collective-permute-done.3.other_ref = bf16[512,32,128]{2,1,0:T(8,128)(2,1)} collective-permute-done((bf16[512,32,128]{2,1,0:T(8,128)(2,1)}, bf16[512,32,128]{2,1,0:T(8,128)(2,1)}, u32[]{:S(2)}, u32[]{:S(2)}) %collective-permute-start.3) | collective-permute-done | bytes 4194336 | tf_op jit(solution)/shard_map/ppermute | solution.py:24
  435.8 20.8 %shard_map.97 = bf16[64,64,1536]{2,1,0:T(8,128)(2,1)} custom-call(f32[1]{0:T(128)} %bitcast.sign_ref, bf16[512,32,128]{2,1,0:T(8,128)(2,1)} %shard_map.96.own_ref, bf16[512,32,128]{2,1,0:T(8,128)(2,1)} %collective-permute-done.3.other_ref, bf16[512,1536]{1,0:T(8,128)(2,1)} %convolution_convert_fusion.1.table_ref, bf16[64,64,1536]{2,1,0:T(8,128)(2,1)} %shard_map.95.refs_1_.refs_0_), custom_call_target="tpu_custom_call" | custom-call | flops 6442450944 | bytes 47710208 | tf_op jit(solution)/shard_map/pallas_call | solution.py:301
  (7 shorter events, 0.1 us)
Async XLA Ops:
  22.8 7.5 %collective-permute-start.1 = (bf16[512,32,128]{2,1,0:T(8,128)(2,1)}, bf16[512,32,128]{2,1,0:T(8,128)(2,1)S(1)}, u32[]{:S(2)}, u32[]{:S(2)}) collective-permute-start(bf16[512,32,128]{2,1,0:T(8,128)(2,1)} %shard_map.93), channel_id=1, source_target_pairs={{0,1},{1,0},{2,3},{3,2},{4,5},{5,4},{6,7},{7,6},{8,9},{9,8},{10,11... | collective-permute-start | bytes 12582920 | tf_op jit(solution)/shard_map/ppermute | solution.py:24
  35.8 7.7 %copy-start.3 = (bf16[1024,1536]{1,0:T(8,128)(2,1)S(1)}, bf16[1024,1536]{1,0:T(8,128)(2,1)}, u32[]{:S(2)}) copy-start(bf16[1024,1536]{1,0:T(8,128)(2,1)} %constant.41.clone) | copy-start | bytes 9437188
  35.8 101.0 %all-to-all-start.2 = ((bf16[8,32,64,128]{3,2,1,0:T(8,128)(2,1)}), bf16[8,32,64,128]{3,2,1,0:T(8,128)(2,1)}, u32[]{:S(2)}, u32[]{:S(2)}) async-start(bf16[8,32,64,128]{3,2,1,0:T(8,128)(2,1)} %bitcast.38), calls=%async_computation.2 | async-start | bytes 8388608 | tf_op jit(solution)/shard_map/all_to_all | solution.py:390
  61.8 7.4 %collective-permute-start = (bf16[512,32,128]{2,1,0:T(8,128)(2,1)}, bf16[512,32,128]{2,1,0:T(8,128)(2,1)S(1)}, u32[]{:S(2)}, u32[]{:S(2)}) collective-permute-start(bf16[512,32,128]{2,1,0:T(8,128)(2,1)} %shard_map.91), channel_id=1, source_target_pairs={{0,1},{1,0},{2,3},{3,2},{4,5},{5,4},{6,7},{7,6},{8,9},{9,8},{10,11... | collective-permute-start | bytes 12582920 | tf_op jit(solution)/shard_map/ppermute | solution.py:24
  136.7 5.7 %copy-start = (bf16[128,128]{1,0:T(8,128)(2,1)S(1)}, bf16[128,128]{1,0:T(8,128)(2,1)}, u32[]{:S(2)}) copy-start(bf16[128,128]{1,0:T(8,128)(2,1)} %param.14) | copy-start | bytes 98308
  136.7 5.8 %copy-start.1 = (bf16[128,128]{1,0:T(8,128)(2,1)S(1)}, bf16[128,128]{1,0:T(8,128)(2,1)}, u32[]{:S(2)}) copy-start(bf16[128,128]{1,0:T(8,128)(2,1)} %param.15) | copy-start | bytes 98308
  136.7 5.8 %copy-start.2 = (f32[128]{0:T(128)S(1)}, f32[128]{0:T(128)}, u32[]{:S(2)}) copy-start(f32[128]{0:T(128)} %param.13) | copy-start | bytes 1540
  136.7 97.3 %all-to-all-start = ((bf16[8,32,64,128]{3,2,1,0:T(8,128)(2,1)}), bf16[8,32,64,128]{3,2,1,0:T(8,128)(2,1)}, u32[]{:S(2)}, u32[]{:S(2)}) async-start(bf16[8,32,64,128]{3,2,1,0:T(8,128)(2,1)} %bitcast.37), calls=%async_computation | async-start | bytes 8388608 | tf_op jit(solution)/shard_map/all_to_all | solution.py:390
  234.1 97.1 %all-to-all-start.3 = ((bf16[8,32,64,128]{3,2,1,0:T(8,128)(2,1)}), bf16[8,32,64,128]{3,2,1,0:T(8,128)(2,1)}, u32[]{:S(2)}, u32[]{:S(2)}) async-start(bf16[8,32,64,128]{3,2,1,0:T(8,128)(2,1)} %bitcast.40), calls=%async_computation.3 | async-start | bytes 8388608 | tf_op jit(solution)/shard_map/all_to_all | solution.py:402
  331.2 97.1 %all-to-all-start.1 = ((bf16[8,32,64,128]{3,2,1,0:T(8,128)(2,1)}), bf16[8,32,64,128]{3,2,1,0:T(8,128)(2,1)}, u32[]{:S(2)}, u32[]{:S(2)}) async-start(bf16[8,32,64,128]{3,2,1,0:T(8,128)(2,1)} %bitcast.39), calls=%async_computation.1 | async-start | bytes 8388608 | tf_op jit(solution)/shard_map/all_to_all | solution.py:402
  335.8 7.6 %collective-permute-start.2 = (bf16[512,32,128]{2,1,0:T(8,128)(2,1)}, bf16[512,32,128]{2,1,0:T(8,128)(2,1)}, u32[]{:S(2)}, u32[]{:S(2)}) collective-permute-start(bf16[512,32,128]{2,1,0:T(8,128)(2,1)} %bitcast.16.own_ref), channel_id=1, source_target_pairs={{0,1},{1,0},{2,3},{3,2},{4,5},{5,4},{6,7},{7,6},{8,9},{9,8},{10,11... | collective-permute-start | bytes 12582920 | tf_op jit(solution)/shard_map/ppermute | solution.py:24
  428.3 7.5 %collective-permute-start.3 = (bf16[512,32,128]{2,1,0:T(8,128)(2,1)}, bf16[512,32,128]{2,1,0:T(8,128)(2,1)}, u32[]{:S(2)}, u32[]{:S(2)}) collective-permute-start(bf16[512,32,128]{2,1,0:T(8,128)(2,1)} %shard_map.96.own_ref), channel_id=1, source_target_pairs={{0,1},{1,0},{2,3},{3,2},{4,5},{5,4},{6,7},{7,6},{8,9},{9,8},{10,11... | collective-permute-start | bytes 12582920 | tf_op jit(solution)/shard_map/ppermute | solution.py:24
